TPU v7x, 128 devices: a whole 4x4x4 slice. The times are simulated.
128 devices in a mesh: tm: 8 (over x, core), sy: 4 (over z), sx: 4 (over y).
Axes of the slice: x: 4, y: 4, z: 4, core: 2. Of those that a mesh axis runs over, the one named last changes fastest.
Arguments:
- latent_init: float32 [64, 96, 320], P('sy', 'sx'), may hold values from -80 to 80
- step_noise: bfloat16 [32, 64, 96, 320], P('tm', 'sy', 'sx'), may hold values from -6 to 6
- coef_state: float32 [32], P('tm'), may hold values from -0.06 to -0.01
- coef_drift: float32 [32], P('tm'), may hold values from -0.1 to 0.1
- coef_noise: float32 [32], P('tm'), may hold values from 0.05 to 0.2
- step_index: int32 [32], P('tm'), may hold values from 0 to 999
- time_table: float32 [1000, 320], replicated, may hold values from -1.5 to 1.5
- norm_gain: float32 [320], replicated, may hold values from 0.25 to 1.75
- conv_weight: bfloat16 [3, 3, 320, 320], replicated, may hold values from -0.109375 to 0.109375
- reward_grad: float32 [64, 96, 320], P('sy', 'sx'), may hold values from -0.18 to 0.18
Outputs:
- trajectory: float32 [32, 64, 96, 320], P('tm', 'sy', 'sx')
- grad_weight: float32 [3, 3, 320, 320], P(None, None, None, 'tm')
All inputs are finite; a program needn't handle non-finite values.
Results may differ from a plain program's by a relative error of at most 0.0009.
The roundings to bfloat16 on the way count: a program that leaves them out, or rounds other values in their place, can miss the bound.
Values may be sent and summed in bfloat16 or wider, within the bound.
A program may use at most 128 MiB of HBM per device.

v0:
```python
import jax
import jax.numpy as jnp
from jax import lax
from jax.sharding import PartitionSpec as P

GROUPS = 32
ITERS = 2
EPSILON = 1e-05


def prefix(value, axis, join, neutral, backward):
    count, mine = (lax.axis_size(axis), lax.axis_index(axis))
    pieces = lax.all_gather(value, axis)
    if backward:
        pieces = pieces[::-1]
        mine = count - 1 - mine
    subtotal = jnp.full_like(value, 0) + jnp.asarray(neutral, value.dtype)

    def step(position, subtotal):
        longer = join(subtotal, pieces[position])
        return jnp.where(position < mine, longer, subtotal)

    return lax.fori_loop(0, count - 1, step, subtotal)


def with_halo(block, sides, width):
    for axis, dim in sides:
        count = lax.axis_size(axis)
        forward = [(i, i + 1) for i in range(count - 1)]
        backward = [(target, source) for source, target in forward]
        low = lax.ppermute(
            lax.slice_in_dim(block, block.shape[dim] - width, None, axis=dim), axis, forward
        )
        high = lax.ppermute(lax.slice_in_dim(block, 0, width, axis=dim), axis, backward)
        block = jnp.concatenate([low, block, high], axis=dim)
    return block


def add_terms(earlier, later):
    return earlier + later


def lower_total(block_total, reverse):
    return prefix(block_total, "tm", add_terms, jnp.zeros_like(block_total), reverse)


def group_count(tile_rows, tile_cols, channels):
    return tile_rows * lax.axis_size("sy") * tile_cols * lax.axis_size("sx") * (channels // GROUPS)


def group_stats(grouped, cell_count):
    totals = lax.psum(jnp.sum(grouped, axis=(1, 3)), ("sy", "sx"))
    center = totals / cell_count
    shifted = grouped - center[:, None, :, None]
    spread = lax.psum(jnp.sum(shifted * shifted, axis=(1, 3)), ("sy", "sx")) / cell_count
    return (shifted, spread)


def prepare(states, modulate):
    steps_here, tile_rows, tile_cols, channels = states.shape
    grouped = states.reshape(steps_here, tile_rows * tile_cols, GROUPS, channels // GROUPS)
    shifted, spread = group_stats(grouped, group_count(tile_rows, tile_cols, channels))
    inv_std = 1.0 / jnp.sqrt(spread + EPSILON)
    normal_field = (shifted * inv_std[:, None, :, None]).reshape(states.shape)
    pre_act = normal_field * modulate[:, None, None, :]
    activation = jax.nn.silu(pre_act).astype(jnp.bfloat16)
    act_pad = with_halo(activation, (("sy", 1), ("sx", 2)), 1)
    return (normal_field, inv_std, pre_act, act_pad)


def convolve(act_pad, conv_weight, tile_rows, tile_cols):
    result = jnp.zeros(
        act_pad.shape[:1] + (tile_rows, tile_cols, conv_weight.shape[3]), jnp.float32
    )
    for row_off in range(3):
        for col_off in range(3):
            window = act_pad[:, row_off : row_off + tile_rows, col_off : col_off + tile_cols, :]
            result = result + jnp.einsum(
                "bhwc,cd->bhwd",
                window,
                conv_weight[row_off, col_off],
                preferred_element_type=jnp.float32,
            )
    return result


def backprop(upstream, act_cache, modulate, conv_weight, need_state):
    normal_field, inv_std, pre_act, act_pad = act_cache
    steps_here, tile_rows, tile_cols, channels = upstream.shape
    up_half = upstream.astype(jnp.bfloat16)
    weight_rows = []
    for row_off in range(3):
        weight_cols = []
        for col_off in range(3):
            window = act_pad[:, row_off : row_off + tile_rows, col_off : col_off + tile_cols, :]
            weight_cols.append(
                jnp.einsum("bhwc,bhwd->cd", window, up_half, preferred_element_type=jnp.float32)
            )
        weight_rows.append(jnp.stack(weight_cols))
    grad_piece = jnp.stack(weight_rows)
    if not need_state:
        return (upstream, grad_piece)
    up_pad = with_halo(up_half, (("sy", 1), ("sx", 2)), 1)
    d_act = jnp.zeros(upstream.shape, jnp.float32)
    for row_off in range(3):
        for col_off in range(3):
            window = up_pad[
                :, 2 - row_off : 2 - row_off + tile_rows, 2 - col_off : 2 - col_off + tile_cols, :
            ]
            d_act = d_act + jnp.einsum(
                "bhwd,cd->bhwc",
                window,
                conv_weight[row_off, col_off],
                preferred_element_type=jnp.float32,
            )
    sig_value = jax.nn.sigmoid(pre_act)
    d_norm = d_act * sig_value * (1.0 + pre_act * (1.0 - sig_value)) * modulate[:, None, None, :]
    group_shape = (steps_here, tile_rows * tile_cols, GROUPS, channels // GROUPS)
    grouped_d = d_norm.reshape(group_shape)
    grouped_n = normal_field.reshape(group_shape)
    cell_count = group_count(tile_rows, tile_cols, channels)
    plain_sum, cross_sum = lax.psum(
        (jnp.sum(grouped_d, axis=(1, 3)), jnp.sum(grouped_d * grouped_n, axis=(1, 3))), ("sy", "sx")
    )
    plain_mean = plain_sum / cell_count
    cross_mean = cross_sum / cell_count
    d_group = (
        grouped_d - plain_mean[:, None, :, None] - grouped_n * cross_mean[:, None, :, None]
    ) * inv_std[:, None, :, None]
    return (upstream + d_group.reshape(upstream.shape), grad_piece)


def shards(
    latent_init,
    step_noise,
    coef_state,
    coef_drift,
    coef_noise,
    step_index,
    time_table,
    norm_gain,
    conv_weight,
    reward_grad,
):
    tile_rows, tile_cols = (step_noise.shape[1], step_noise.shape[2])
    table_ids = jnp.arange(time_table.shape[0], dtype=jnp.int32)
    one_hot = (step_index[:, None] == table_ids[None, :]).astype(jnp.float32)
    embedded = jnp.dot(one_hot, time_table, precision=lax.Precision.HIGHEST)
    modulate = norm_gain[None, :] * (1.0 + embedded)
    state_c = coef_state[:, None, None, None]
    drift_c = coef_drift[:, None, None, None]
    noise_c = coef_noise[:, None, None, None]
    states = jnp.broadcast_to(latent_init[None], step_noise.shape)
    saved_states = []
    caches = []
    trajectory = states
    for sweep_index in range(ITERS):
        saved_states.append(states)
        act_cache = prepare(states, modulate)
        caches.append(act_cache)
        drift_term = states + convolve(act_cache[3], conv_weight, tile_rows, tile_cols)
        increment = (
            state_c * states + drift_c * drift_term + noise_c * step_noise.astype(jnp.float32)
        )
        running = jnp.cumsum(increment, axis=0)
        offset = lower_total(running[-1], False)
        trajectory = latent_init[None] + (offset[None] + running)
        if sweep_index + 1 < ITERS:
            before = jnp.concatenate([jnp.zeros_like(running[:1]), running[:-1]], axis=0)
            states = latent_init[None] + (offset[None] + before)
    adjoint = jnp.broadcast_to(reward_grad[None], step_noise.shape)
    grad_total = jnp.zeros(conv_weight.shape, jnp.float32)
    for sweep_index in range(ITERS - 1, -1, -1):
        act_cache = prepare(saved_states[sweep_index], modulate)
        upstream = drift_c * adjoint
        d_state, grad_piece = backprop(upstream, act_cache, modulate, conv_weight, sweep_index > 0)
        grad_total = grad_total + grad_piece
        if sweep_index > 0:
            through = state_c * adjoint + d_state
            suffix = jnp.cumsum(through[::-1], axis=0)[::-1]
            higher = lower_total(suffix[0], True)
            after = jnp.concatenate([suffix[1:], jnp.zeros_like(suffix[:1])], axis=0)
            adjoint = higher[None] + after
    share = lax.psum_scatter(grad_total, "tm", scatter_dimension=3, tiled=True)
    grad_weight = lax.psum(share, ("sy", "sx"))
    return (trajectory, grad_weight)


def solution(mesh):
    placed = (
        P("sy", "sx", None),
        P("tm", "sy", "sx", None),
        P("tm"),
        P("tm"),
        P("tm"),
        P("tm"),
        P(),
        P(),
        P(),
        P("sy", "sx", None),
    )
    return jax.shard_map(
        shards,
        mesh=mesh,
        in_specs=placed,
        out_specs=(P("tm", "sy", "sx", None), P(None, None, None, "tm")),
        check_vma=False,
    )
```

profile of v0, /device:TPU:0, one launch (start us, length us, event | category | flops | bytes accessed | tf_op | source)
XLA Modules:
  0.0 634.3 jit_solution(18137577999258617183)
XLA Ops:
  8.7 42.0 %psum.46 = f32[4,32]{1,0:T(4,128)S(1)} all-reduce(f32[4,32]{1,0:T(4,128)S(1)} %reduce_sum.117), channel_id=1, replica_groups=mesh['tm'=8,'sy'=4,'sx'=4] {'sy','sx'}, use_global_device_ids=true, to_apply=%region_2.0 | all-reduce | flops 128 | bytes 1024 | tf_op jit(solution)/shard_map/psum | solution.py:52
  52.5 35.5 %psum.49 = f32[4,32]{1,0:T(4,128)S(1)} all-reduce(f32[4,32]{1,0:T(4,128)S(1)} %reduce_sum.120), channel_id=1, replica_groups=mesh['tm'=8,'sy'=4,'sx'=4] {'sy','sx'}, use_global_device_ids=true, to_apply=%region_5.6 | all-reduce | flops 128 | bytes 1024 | tf_op jit(solution)/shard_map/psum | solution.py:55
  98.3 3.9 collective-permute-start.2
  123.3 6.3 fusion.33
  135.9 3.3 fusion
  142.3 4.7 collective-permute-start.11
  147.1 3.3 fusion.48
  166.6 8.7 %while.42 = (s32[]{:T(128)}, f32[16,24,320]{2,1,0:T(8,128)S(1)}, s32[]{:T(128)}, f32[8,16,24,320]{3,2,1,0:T(8,128)}, s32[]{:T(128)}, /*index=5*/s32[]{:T(128)}) while((s32[]{:T(128)}, f32[16,24,320]{2,1,0:T(8,128)S(1)}, s32[]{:T(128)}, f32[8,16,24,320]{3,2,1,0:T(8,128)}, s32[]{:T(128)}, /*index=5*/s32[]{:T(128)}) %tuple.106), condition=%wide.region_8.9_spmd.clone, body=%wide.region_7.8_spmd.clone.sunk | while | flops 368644 | bytes 1474653 | solution.py:23
  177.3 39.5 %psum.50 = f32[4,32]{1,0:T(4,128)S(1)} all-reduce(f32[4,32]{1,0:T(4,128)S(1)} %reduce_sum.123), channel_id=1, replica_groups=mesh['tm'=8,'sy'=4,'sx'=4] {'sy','sx'}, use_global_device_ids=true, to_apply=%region_11.12 | all-reduce | flops 128 | bytes 1024 | tf_op jit(solution)/shard_map/psum | solution.py:52
  222.4 36.1 %psum.51 = f32[4,32]{1,0:T(4,128)} all-reduce(f32[4,32]{1,0:T(4,128)} %reduce_sum.126), channel_id=1, replica_groups=mesh['tm'=8,'sy'=4,'sx'=4] {'sy','sx'}, use_global_device_ids=true, to_apply=%region_14.15 | all-reduce | flops 128 | bytes 1024 | tf_op jit(solution)/shard_map/psum | solution.py:55
  261.5 11.5 %fusion.219 = (f32[4,320]{1,0:T(4,128)}, f32[4,320]{1,0:T(4,128)}, f32[4,16,24,320]{3,2,1,0:T(8,128)}) fusion(f32[4,320]{1,0:T(4,128)} %mul.201, f32[4,320]{1,0:T(4,128)S(1)} %sub.66, f32[3,16,24,320]{3,2,1,0:T(8,128)S(1)} %slice.280, f32[16,24,320]{2,1,0:T(8,128)S(1)} %get-tuple-element.239, f32[16,24,320]{2,1,0:T(8,128)S(1)} %copy-done.2, ...), kind=kOutput, calls=%fused_computation.276 | convolution fusion | flops 326858240 | bytes 24750080 | tf_op jit(solution)/shard_map/bhwd,cd->bhwc/dot_general | solution.py:110
  278.9 38.4 %all-reduce.3 = (f32[4,32]{1,0:T(4,128)}, f32[4,32]{1,0:T(4,128)}) all-reduce(f32[4,32]{1,0:T(4,128)} %reduce_sum.132, f32[4,32]{1,0:T(4,128)} %reduce_sum.129), channel_id=1, replica_groups=mesh['tm'=8,'sy'=4,'sx'=4] {'sy','sx'}, use_global_device_ids=true, to_apply=%region_23.24 | all-reduce | flops 256 | bytes 2048 | tf_op jit(solution)/shard_map/psum | solution.py:122
  323.7 5.2 fusion.18
  328.9 3.3 rev.7
  344.5 3.5 fusion.162
  356.8 3.8 fusion.146
  363.9 3.3 fusion.145
  378.1 3.4 fusion.110
  381.5 4.9 rev.8
  386.4 8.7 %while.44 = (s32[]{:T(128)}, f32[16,24,320]{2,1,0:T(8,128)S(1)}, s32[]{:T(128)}, f32[8,16,24,320]{3,2,1,0:T(8,128)}, s32[]{:T(128)}, /*index=5*/s32[]{:T(128)}) while((s32[]{:T(128)}, f32[16,24,320]{2,1,0:T(8,128)S(1)}, s32[]{:T(128)}, f32[8,16,24,320]{3,2,1,0:T(8,128)}, s32[]{:T(128)}, /*index=5*/s32[]{:T(128)}) %tuple.112), condition=%wide.region_26.27_spmd.clone, body=%wide.region_25.26_spmd.clone.sunk | while | flops 368644 | bytes 1474653 | solution.py:23
  410.1 8.4 %copy.14 = f32[3,3,320,320]{2,1,0,3:T(4,128)} copy(f32[3,3,320,320]{3,2,1,0:T(8,128)} %maximum_add_fusion) | data formatting | bytes 7372800 | tf_op jit(solution)/shard_map/add | solution.py:177
  419.1 3.9 fusion.113
  423.0 3.6 fusion.116
  426.6 3.4 fusion.119
  430.0 3.5 fusion.122
  433.5 3.4 fusion.125
  436.9 8.6 %fusion.19 = f32[4,16,24,320]{3,2,1,0:T(8,128)S(1)} fusion(f32[4,16,24,320]{3,2,1,0:T(8,128)} %fusion.110, f32[4,16,24,320]{3,2,1,0:T(8,128)} %fusion.145, f32[4,16,24,320]{3,2,1,0:T(8,128)} %fusion.113, f32[4,16,24,320]{3,2,1,0:T(8,128)} %fusion.116, f32[4,16,24,320]{3,2,1,0:T(8,128)} %fusion.162, f32[4,16,24,320]{3,2,1,0:T(8,128)} %fusion.119, ...), kind=kOutput, calls=%fused_computation.31 | output fusion | flops 9830400 | bytes 23101488 | tf_op jit(solution)/shard_map/jit(cumsum)/reduce_window_sum | solution.py:165
  449.1 50.9 %all-reduce.9.cloned.1.call-done = f32[3,3,320,320]{2,1,0,3:T(4,128)} async-done(((f32[3,3,320,320]{2,1,0,3:T(4,128)}), f32[3,3,320,320]{2,1,0,3:T(4,128)}) %all-reduce.9.cloned.1.call-update) | async-done | bytes 3686416
  502.2 33.7 %all-gather.6.cloned.1.call-done = f32[8,16,24,320]{3,2,1,0:T(8,128)} async-done(((f32[1,16,24,320]{3,2,1,0:T(8,128)}), f32[8,16,24,320]{3,2,1,0:T(8,128)}) %all-gather.6.cloned.1.call-update) | async-done | bytes 3932176 | tf_op jit(solution)/shard_map/all_gather | solution.py:13
  535.9 8.7 %while.43 = (s32[]{:T(128)}, f32[16,24,320]{2,1,0:T(8,128)S(1)}, s32[]{:T(128)}, f32[8,16,24,320]{3,2,1,0:T(8,128)}, s32[]{:T(128)}, /*index=5*/s32[]{:T(128)}) while((s32[]{:T(128)}, f32[16,24,320]{2,1,0:T(8,128)S(1)}, s32[]{:T(128)}, f32[8,16,24,320]{3,2,1,0:T(8,128)}, s32[]{:T(128)}, /*index=5*/s32[]{:T(128)}) %tuple.109), condition=%wide.region_17.18_spmd.clone, body=%wide.region_16.17_spmd.clone.sunk | while | flops 368644 | bytes 1474653 | solution.py:23
  544.6 3.4 add_add_fusion
  548.0 77.7 %all-reduce.7.cloned.1.call-done = f32[3,3,320,40]{2,1,0,3:T(4,128)} async-done(((f32[3,3,320,40]{2,1,0,3:T(4,128)}), f32[3,3,320,40]{2,1,0,3:T(4,128)}) %all-reduce.7.cloned.1.call-update) | async-done | bytes 460816 | tf_op jit(solution)/shard_map/psum | solution.py:185
  (255 shorter events, 166.0 us)
Async XLA Ops:
  7.2 81.0 %copy-start = (f32[1000,320]{0,1:T(8,128)S(1)}, f32[1000,320]{0,1:T(8,128)}, u32[]{:S(2)}) copy-start(f32[1000,320]{0,1:T(8,128)} %param.22) | copy-start | bytes 3840004
  7.2 82.6 %copy-start.2 = (f32[16,24,320]{2,1,0:T(8,128)S(1)}, f32[16,24,320]{2,1,0:T(8,128)}, u32[]{:S(2)}) copy-start(f32[16,24,320]{2,1,0:T(8,128)} %param.16) | copy-start | bytes 1474564
  7.2 159.4 %all-gather.4.cloned.1.call-start = ((), (), s32[]{:S(2)}) async-start(), calls=%async_computation | async-start | bytes 5308416 | tf_op jit(solution)/shard_map/all_gather | solution.py:13
  51.0 44.8 %copy-start.39 = (f32[4,320]{1,0:T(4,128)}, f32[4,320]{1,0:T(4,128)S(1)}, u32[]{:S(2)}) copy-start(f32[4,320]{1,0:T(4,128)S(1)} %sub.62) | copy-start | bytes 15364
  90.5 18.4 %copy-start.5 = (bf16[4,16,24,320]{3,2,1,0:T(8,128)(2,1)}, bf16[4,16,24,320]{3,2,1,0:T(8,128)(2,1)S(1)}, u32[]{:S(2)}) copy-start(bf16[4,16,24,320]{3,2,1,0:T(8,128)(2,1)S(1)} %fusion.17) | copy-start | bytes 2949124
  90.5 5.2 collective-permute-start
  91.8 6.2 collective-permute-start.1
  95.8 13.1 %copy-start.32 = (bf16[4,1,24,320]{3,2,1,0:T(8,128)(2,1)}, bf16[4,1,24,320]{3,2,1,0:T(8,128)(2,1)S(1)}, u32[]{:S(2)}) copy-start(bf16[4,1,24,320]{3,2,1,0:T(8,128)(2,1)S(1)} %collective-permute-done) | copy-start | bytes 184324
  98.1 10.8 %copy-start.30 = (bf16[4,1,24,320]{3,2,1,0:T(8,128)(2,1)}, bf16[4,1,24,320]{3,2,1,0:T(8,128)(2,1)S(1)}, u32[]{:S(2)}) copy-start(bf16[4,1,24,320]{3,2,1,0:T(8,128)(2,1)S(1)} %collective-permute-done.1) | copy-start | bytes 184324
  98.3 7.8 %collective-permute-start.2 = (bf16[4,18,1,320]{3,2,1,0:T(2,128)(2,1)S(1)}, bf16[4,18,1,320]{3,2,1,0:T(2,128)(2,1)S(1)}, u32[]{:S(2)}, u32[]{:S(2)}) collective-permute-start(bf16[4,18,1,320]{3,2,1,0:T(2,128)(2,1)S(1)} %get-tuple-element.333), channel_id=1, source_target_pairs={{0,1},{1,2},{2,3},{4,5},{5,6},{6,7},{8,9},{9,10},{10,11},{12,13},{... | collective-permute-start | bytes 138248 | tf_op jit(solution)/shard_map/ppermute | solution.py:31
  102.2 6.6 %collective-permute-start.3 = (bf16[4,18,1,320]{3,2,1,0:T(2,128)(2,1)S(1)}, bf16[4,18,1,320]{3,2,1,0:T(2,128)(2,1)S(1)}, u32[]{:S(2)}, u32[]{:S(2)}) collective-permute-start(bf16[4,18,1,320]{3,2,1,0:T(2,128)(2,1)S(1)} %get-tuple-element.334), channel_id=1, source_target_pairs={{1,0},{2,1},{3,2},{5,4},{6,5},{7,6},{9,8},{10,9},{11,10},{13,12},{... | collective-permute-start | bytes 138248 | tf_op jit(solution)/shard_map/ppermute | solution.py:34
  110.0 10.8 %copy-start.13 = (bf16[4,18,25,320]{3,2,1,0:T(8,128)(2,1)}, bf16[4,18,25,320]{3,2,1,0:T(8,128)(2,1)S(1)}, u32[]{:S(2)}) copy-start(bf16[4,18,25,320]{3,2,1,0:T(8,128)(2,1)S(1)} %get-tuple-element.331) | copy-start | bytes 3456004
  123.3 8.7 %copy-start.28 = (f32[16,24,320]{2,1,0:T(8,128)S(1)}, f32[16,24,320]{2,1,0:T(8,128)}, u32[]{:S(2)}) copy-start(f32[16,24,320]{2,1,0:T(8,128)} %param.25) | copy-start | bytes 1474564
  131.9 249.6 %all-gather.8.cloned.1.call-start = ((), (), s32[]{:S(2)}) async-start(), calls=%async_computation.2 | async-start | bytes 5308416 | tf_op jit(solution)/shard_map/all_gather | solution.py:13
  132.3 18.0 %copy-start.7 = (bf16[4,16,24,320]{3,2,1,0:T(8,128)(2,1)}, bf16[4,16,24,320]{3,2,1,0:T(8,128)(2,1)S(1)}, u32[]{:S(2)}) copy-start(bf16[4,16,24,320]{3,2,1,0:T(8,128)(2,1)S(1)} %multiply_convert_fusion) | copy-start | bytes 2949124
  132.3 6.9 %collective-permute-start.8 = (bf16[4,1,24,320]{3,2,1,0:T(8,128)(2,1)S(1)}, bf16[4,1,24,320]{3,2,1,0:T(8,128)(2,1)S(1)}, u32[]{:S(2)}, u32[]{:S(2)}) collective-permute-start(bf16[4,1,24,320]{3,2,1,0:T(8,128)(2,1)S(1)} %get-tuple-element.336), channel_id=1, source_target_pairs={{0,4},{4,8},{8,12},{1,5},{5,9},{9,13},{2,6},{6,10},{10,14},{3,7},{... | collective-permute-start | bytes 184328 | tf_op jit(solution)/shard_map/ppermute | solution.py:31
  134.6 6.2 collective-permute-start.9
  139.2 11.1 %copy-start.10 = (bf16[3,3,320,320]{3,2,1,0:T(8,128)(2,1)S(1)}, bf16[3,3,320,320]{3,2,1,0:T(8,128)(2,1)}, u32[]{:S(2)}) copy-start(bf16[3,3,320,320]{3,2,1,0:T(8,128)(2,1)} %param.24) | copy-start | bytes 5529604
  139.2 11.1 %copy-start.34 = (bf16[4,1,24,320]{3,2,1,0:T(8,128)(2,1)}, bf16[4,1,24,320]{3,2,1,0:T(8,128)(2,1)S(1)}, u32[]{:S(2)}) copy-start(bf16[4,1,24,320]{3,2,1,0:T(8,128)(2,1)S(1)} %collective-permute-done.8) | copy-start | bytes 184324
  140.8 9.5 %copy-start.36 = (bf16[4,1,24,320]{3,2,1,0:T(8,128)(2,1)}, bf16[4,1,24,320]{3,2,1,0:T(8,128)(2,1)S(1)}, u32[]{:S(2)}) copy-start(bf16[4,1,24,320]{3,2,1,0:T(8,128)(2,1)S(1)} %collective-permute-done.9) | copy-start | bytes 184324
  141.0 11.8 %collective-permute-start.10 = (bf16[4,18,1,320]{3,2,1,0:T(2,128)(2,1)S(1)}, bf16[4,18,1,320]{3,2,1,0:T(2,128)(2,1)S(1)}, u32[]{:S(2)}, u32[]{:S(2)}) collective-permute-start(bf16[4,18,1,320]{3,2,1,0:T(2,128)(2,1)S(1)} %get-tuple-element.326), channel_id=1, source_target_pairs={{1,0},{2,1},{3,2},{5,4},{6,5},{7,6},{9,8},{10,9},{11,10},{13,12},{... | collective-permute-start | bytes 138248 | tf_op jit(solution)/shard_map/ppermute | solution.py:34
  142.3 10.5 %collective-permute-start.11 = (bf16[4,18,1,320]{3,2,1,0:T(2,128)(2,1)S(1)}, bf16[4,18,1,320]{3,2,1,0:T(2,128)(2,1)S(1)}, u32[]{:S(2)}, u32[]{:S(2)}) collective-permute-start(bf16[4,18,1,320]{3,2,1,0:T(2,128)(2,1)S(1)} %get-tuple-element.325), channel_id=1, source_target_pairs={{0,1},{1,2},{2,3},{4,5},{5,6},{6,7},{8,9},{9,10},{10,11},{12,13},{... | collective-permute-start | bytes 138248 | tf_op jit(solution)/shard_map/ppermute | solution.py:31
  332.1 9.1 %copy-start.44 = (f32[4]{0:T(128)S(1)}, f32[4]{0:T(128)}, u32[]{:S(2)}) copy-start(f32[4]{0:T(128)} %param.19) | copy-start | bytes 52
  336.3 163.8 %all-reduce.9.cloned.1.call-start = ((), (), s32[]{:S(2)}) async-start(), calls=%async_computation.4 | async-start | bytes 11796480
  337.9 14.2 %collective-permute-start.4 = (bf16[4,1,24,320]{3,2,1,0:T(8,128)(2,1)}, bf16[4,1,24,320]{3,2,1,0:T(8,128)(2,1)}, u32[]{:S(2)}, u32[]{:S(2)}) collective-permute-start(bf16[4,1,24,320]{3,2,1,0:T(8,128)(2,1)} %get-tuple-element.337), channel_id=1, source_target_pairs={{0,4},{4,8},{8,12},{1,5},{5,9},{9,13},{2,6},{6,10},{10,14},{3,7},{... | collective-permute-start | bytes 184328 | tf_op jit(solution)/shard_map/ppermute | solution.py:31
  339.8 12.3 %collective-permute-start.5 = (bf16[4,1,24,320]{3,2,1,0:T(8,128)(2,1)}, bf16[4,1,24,320]{3,2,1,0:T(8,128)(2,1)}, u32[]{:S(2)}, u32[]{:S(2)}) collective-permute-start(bf16[4,1,24,320]{3,2,1,0:T(8,128)(2,1)} %get-tuple-element.338), channel_id=1, source_target_pairs={{4,0},{8,4},{12,8},{5,1},{9,5},{13,9},{6,2},{10,6},{14,10},{7,3},{... | collective-permute-start | bytes 184328 | tf_op jit(solution)/shard_map/ppermute | solution.py:34
  353.7 13.6 %collective-permute-start.6 = (bf16[4,18,1,320]{3,2,1,0:T(2,128)(2,1)S(1)}, bf16[4,18,1,320]{3,2,1,0:T(2,128)(2,1)S(1)}, u32[]{:S(2)}, u32[]{:S(2)}) collective-permute-start(bf16[4,18,1,320]{3,2,1,0:T(2,128)(2,1)S(1)} %get-tuple-element.329), channel_id=1, source_target_pairs={{0,1},{1,2},{2,3},{4,5},{5,6},{6,7},{8,9},{9,10},{10,11},{12,13},{... | collective-permute-start | bytes 138248 | tf_op jit(solution)/shard_map/ppermute | solution.py:31
  355.5 11.8 %collective-permute-start.7 = (bf16[4,18,1,320]{3,2,1,0:T(2,128)(2,1)S(1)}, bf16[4,18,1,320]{3,2,1,0:T(2,128)(2,1)S(1)}, u32[]{:S(2)}, u32[]{:S(2)}) collective-permute-start(bf16[4,18,1,320]{3,2,1,0:T(2,128)(2,1)S(1)} %get-tuple-element.330), channel_id=1, source_target_pairs={{1,0},{2,1},{3,2},{5,4},{6,5},{7,6},{9,8},{10,9},{11,10},{13,12},{... | collective-permute-start | bytes 138248 | tf_op jit(solution)/shard_map/ppermute | solution.py:34
  418.5 117.4 %all-gather.6.cloned.1.call-start = ((), (), s32[]{:S(2)}) async-start(), calls=%async_computation.1 | async-start | bytes 5308416 | tf_op jit(solution)/shard_map/all_gather | solution.py:13
  436.9 11.0 %copy-start.49 = (u32[128]{0:T(128)S(1)}, u32[128]{0:T(128)}, u32[]{:S(2)}) copy-start(u32[128]{0:T(128)} %constant.115) | copy-start | bytes 1540
  447.8 177.9 %all-reduce.7.cloned.1.call-start = ((), (), s32[]{:S(2)}) async-start(), calls=%async_computation.3 | async-start | bytes 1474560 | tf_op jit(solution)/shard_map/psum | solution.py:185
  544.6 83.0 %copy-start.1 = (f32[1000,320]{0,1:T(8,128)S(1)}, f32[1000,320]{0,1:T(8,128)}, u32[]{:S(2)}) copy-start(f32[1000,320]{0,1:T(8,128)} %param.22) | copy-start | bytes 3840004
  (35 other events, 114.0 us)
Sparse Core Ops, SparseCore 0:
  132.0 33.4 all-gather.3
  336.4 29.2 all-gather.7
  418.7 81.3 all-reduce.8
  501.7 34.1 all-gather.5
  539.4 86.2 all-reduce.6
where the time goes:
time: 641 us; the launch traced here: 634 us
  blocking collectives  191 us (30%)
  waiting for transfers between devices  169 us (26%)
  matrix products  101 us (16%)
  other arithmetic  78.4 us (12%)
  local copies, waits for them, and re-layouts  53.7 us (8%)
  starting transfers between devices  24.9 us (4%)
  between operations  15.4 us (2%)
    psum x2, blocking collectives, group_stats(): totals = lax.psum(jnp.sum(grouped, axis=(1, 3)), ('sy', 'sx'))  81.5 us
    psum x1, waiting for transfers between devices, shards(): grad_weight = lax.psum(share, ('sy', 'sx'))  77.7 us
    psum x2, blocking collectives, group_stats(): lax.psum(jnp.sum(shifted * shifted, axis=(1, 3)), ('sy', 'sx')) / cell_count  71.6 us
    unnamed x6, waiting for transfers between devices  51 us
    dot_general x18, matrix products, convolve(): jnp.einsum('bhwc,cd->bhwd', window, conv_weight[row_off, col_off], prefer...  49.6 us
    psum x1, blocking collectives, backprop(): lax.psum((jnp.sum(grouped_d, axis=(1, 3)), jnp.sum(grouped_d * grouped_n,...  38.4 us
    all_gather x3, waiting for transfers between devices, prefix(): pieces = lax.all_gather(value, axis)  33.7 us
    dot_general x9, matrix products, backprop(): jnp.einsum('bhwd,cd->bhwc', window, conv_weight[row_off, col_off], prefer...  31.9 us
  transfers between devices with their start and end apart: 17, of which 6 were waited for; matrix products, arithmetic and copies ran while one was open for 17% of the time, Pallas kernels for 0%

commit v1 on v0

--- a/solution.py
+++ b/solution.py
@@ -6,6 +6,11 @@
 GROUPS = 32
 ITERS = 2
 EPSILON = 1e-05
+
+
+def load_the_streams(page):
+    block_last = lax.psum(page, axis_name="sy")
+    return lax.psum(block_last, axis_name="sx")
 
 
 def prefix(value, axis, join, neutral, backward):
@@ -52,7 +57,7 @@
     totals = lax.psum(jnp.sum(grouped, axis=(1, 3)), ("sy", "sx"))
     center = totals / cell_count
     shifted = grouped - center[:, None, :, None]
-    spread = lax.psum(jnp.sum(shifted * shifted, axis=(1, 3)), ("sy", "sx")) / cell_count
+    spread = load_the_streams(jnp.sum(shifted * shifted, axis=(1, 3))) / cell_count
     return (shifted, spread)
 
 

time: 641 us -> 605 us (0.944)
  blocking collectives: 191 us -> 153 us
    psum x2 -> x4, blocking collectives: 71.6 us -> 32.9 us  [the longest x2 16.7 us: load_the_streams(): return lax.psum(block_last, axis_name='sx')]
  transfers between devices with their start and end apart: 17 -> 17, of which waited for: 6 -> 6; matrix products, arithmetic and copies ran while one was open for 17% -> 18% of each run, Pallas kernels for 0% -> 0%
where the time goes in v1:
time: 605 us; the launch traced here: 598 us
  waiting for transfers between devices  170 us (28%)
  blocking collectives  153 us (25%)
  matrix products  101 us (17%)
  other arithmetic  78.5 us (13%)
  local copies, waits for them, and re-layouts  53.6 us (9%)
  starting transfers between devices  26.5 us (4%)
  between operations  15.5 us (3%)
    psum x2, blocking collectives, group_stats(): totals = lax.psum(jnp.sum(grouped, axis=(1, 3)), ('sy', 'sx'))  80.4 us
    psum x1, waiting for transfers between devices, shards(): grad_weight = lax.psum(share, ('sy', 'sx'))  77.7 us
    unnamed x6, waiting for transfers between devices  51.7 us
    dot_general x18, matrix products, convolve(): jnp.einsum('bhwc,cd->bhwd', window, conv_weight[row_off, col_off], prefer...  49.5 us
    psum x1, blocking collectives, backprop(): lax.psum((jnp.sum(grouped_d, axis=(1, 3)), jnp.sum(grouped_d * grouped_n,...  39.5 us
    all_gather x3, waiting for transfers between devices, prefix(): pieces = lax.all_gather(value, axis)  33.7 us
    dot_general x9, matrix products, backprop(): jnp.einsum('bhwd,cd->bhwc', window, conv_weight[row_off, col_off], prefer...  31.9 us
    select_n x21, other arithmetic, step(): return jnp.where(position < mine, longer, subtotal)  25.6 us
  transfers between devices with their start and end apart: 17, of which 6 were waited for; matrix products, arithmetic and copies ran while one was open for 18% of the time, Pallas kernels for 0%

profile of v1, /device:TPU:0, one launch (start us, length us, event | category | flops | bytes accessed | tf_op | source)
XLA Modules:
  0.0 597.8 jit_solution(12280209810786141959)
XLA Ops:
  8.7 42.0 %psum.60 = f32[4,32]{1,0:T(4,128)S(1)} all-reduce(f32[4,32]{1,0:T(4,128)S(1)} %reduce_sum.117), channel_id=1, replica_groups=mesh['tm'=8,'sy'=4,'sx'=4] {'sy','sx'}, use_global_device_ids=true, to_apply=%region_2.0 | all-reduce | flops 128 | bytes 1024 | tf_op jit(solution)/shard_map/psum | solution.py:57
  52.5 7.7 %psum.61 = f32[4,32]{1,0:T(4,128)S(1)} all-reduce(f32[4,32]{1,0:T(4,128)S(1)} %reduce_sum.120), channel_id=1, replica_groups=mesh['tm'=8,'sy'=4,'sx'=4] {'sy'}, use_global_device_ids=true, to_apply=%region_5.6 | all-reduce | flops 128 | bytes 1024 | tf_op jit(solution)/shard_map/psum | solution.py:12
  60.3 8.0 %psum.64 = f32[4,32]{1,0:T(4,128)S(1)} all-reduce(f32[4,32]{1,0:T(4,128)S(1)} %psum.61), channel_id=1, replica_groups=mesh['tm'=8,'sy'=4,'sx'=4] {'sx'}, use_global_device_ids=true, to_apply=%region_6.7 | all-reduce | flops 128 | bytes 1024 | tf_op jit(solution)/shard_map/psum | solution.py:13
  70.8 3.6 collective-permute-start
  80.9 3.9 collective-permute-start.2
  105.9 6.3 %fusion.33 = f32[4,16,24,320]{3,2,1,0:T(8,128)S(1)} fusion(bf16[4,16,24,320]{3,2,1,0:T(8,128)(2,1)} %param.17, f32[4,16,24,320]{3,2,1,0:T(8,128)S(1)} %fusion.128, f32[4,16,24,320]{3,2,1,0:T(8,128)S(1)} %fusion.147, f32[4,16,24,320]{3,2,1,0:T(8,128)} %fusion.131, f32[4,16,24,320]{3,2,1,0:T(8,128)} %fusion.134, f32[4,16,24,320]{3,2,1,0:T(8,128)} %fusion.164, ...), kind=kOutput, calls=%fused_computation.49 | output fusion | flops 8847360 | bytes 21135408 | tf_op jit(solution)/shard_map/jit(cumsum)/reduce_window_sum | solution.py:170
  125.0 4.7 collective-permute-start.11
  149.2 8.7 %while.42 = (s32[]{:T(128)}, f32[16,24,320]{2,1,0:T(8,128)S(1)}, s32[]{:T(128)}, f32[8,16,24,320]{3,2,1,0:T(8,128)}, s32[]{:T(128)}, /*index=5*/s32[]{:T(128)}) while((s32[]{:T(128)}, f32[16,24,320]{2,1,0:T(8,128)S(1)}, s32[]{:T(128)}, f32[8,16,24,320]{3,2,1,0:T(8,128)}, s32[]{:T(128)}, /*index=5*/s32[]{:T(128)}) %tuple.106), condition=%wide.region_9.10_spmd.clone, body=%wide.region_8.9_spmd.clone.sunk | while | flops 368644 | bytes 1474653 | solution.py:28
  159.8 38.4 %psum.65 = f32[4,32]{1,0:T(4,128)S(1)} all-reduce(f32[4,32]{1,0:T(4,128)S(1)} %reduce_sum.123), channel_id=1, replica_groups=mesh['tm'=8,'sy'=4,'sx'=4] {'sy','sx'}, use_global_device_ids=true, to_apply=%region_12.13 | all-reduce | flops 128 | bytes 1024 | tf_op jit(solution)/shard_map/psum | solution.py:57
  203.9 8.4 %psum.66 = f32[4,32]{1,0:T(4,128)} all-reduce(f32[4,32]{1,0:T(4,128)} %reduce_sum.126), channel_id=1, replica_groups=mesh['tm'=8,'sy'=4,'sx'=4] {'sy'}, use_global_device_ids=true, to_apply=%region_15.16 | all-reduce | flops 128 | bytes 1024 | tf_op jit(solution)/shard_map/psum | solution.py:12
  212.3 8.7 %psum.69 = f32[4,32]{1,0:T(4,128)} all-reduce(f32[4,32]{1,0:T(4,128)} %psum.66), channel_id=1, replica_groups=mesh['tm'=8,'sy'=4,'sx'=4] {'sx'}, use_global_device_ids=true, to_apply=%region_16.17 | all-reduce | flops 128 | bytes 1024 | tf_op jit(solution)/shard_map/psum | solution.py:13
  224.0 11.5 %fusion.219 = (f32[4,320]{1,0:T(4,128)}, f32[4,320]{1,0:T(4,128)}, f32[4,16,24,320]{3,2,1,0:T(8,128)}) fusion(f32[4,320]{1,0:T(4,128)} %mul.201, f32[4,320]{1,0:T(4,128)S(1)} %sub.66, f32[3,16,24,320]{3,2,1,0:T(8,128)S(1)} %slice.280, f32[16,24,320]{2,1,0:T(8,128)S(1)} %get-tuple-element.239, f32[16,24,320]{2,1,0:T(8,128)S(1)} %copy-done.2, ...), kind=kOutput, calls=%fused_computation.276 | convolution fusion | flops 326858240 | bytes 24750080 | tf_op jit(solution)/shard_map/bhwd,cd->bhwc/dot_general | solution.py:115
  241.3 39.5 %all-reduce.3 = (f32[4,32]{1,0:T(4,128)}, f32[4,32]{1,0:T(4,128)}) all-reduce(f32[4,32]{1,0:T(4,128)} %reduce_sum.132, f32[4,32]{1,0:T(4,128)} %reduce_sum.129), channel_id=1, replica_groups=mesh['tm'=8,'sy'=4,'sx'=4] {'sy','sx'}, use_global_device_ids=true, to_apply=%region_25.26 | all-reduce | flops 256 | bytes 2048 | tf_op jit(solution)/shard_map/psum | solution.py:127
  287.3 5.2 fusion.18
  308.2 3.5 fusion.162
  319.9 3.8 fusion.146
  327.0 3.4 fusion.145
  341.4 3.4 fusion.110
  344.8 4.9 rev.8
  349.7 8.7 %while.44 = (s32[]{:T(128)}, f32[16,24,320]{2,1,0:T(8,128)S(1)}, s32[]{:T(128)}, f32[8,16,24,320]{3,2,1,0:T(8,128)}, s32[]{:T(128)}, /*index=5*/s32[]{:T(128)}) while((s32[]{:T(128)}, f32[16,24,320]{2,1,0:T(8,128)S(1)}, s32[]{:T(128)}, f32[8,16,24,320]{3,2,1,0:T(8,128)}, s32[]{:T(128)}, /*index=5*/s32[]{:T(128)}) %tuple.112), condition=%wide.region_28.29_spmd.clone, body=%wide.region_27.28_spmd.clone.sunk | while | flops 368644 | bytes 1474653 | solution.py:28
  373.3 8.4 %copy.14 = f32[3,3,320,320]{2,1,0,3:T(4,128)} copy(f32[3,3,320,320]{3,2,1,0:T(8,128)} %maximum_add_fusion) | data formatting | bytes 7372800 | tf_op jit(solution)/shard_map/add | solution.py:182
  382.0 3.9 fusion.113
  385.9 3.5 fusion.116
  389.4 3.4 fusion.119
  392.8 3.5 fusion.122
  396.3 3.4 fusion.125
  399.7 8.6 %fusion.19 = f32[4,16,24,320]{3,2,1,0:T(8,128)S(1)} fusion(f32[4,16,24,320]{3,2,1,0:T(8,128)} %fusion.110, f32[4,16,24,320]{3,2,1,0:T(8,128)} %fusion.145, f32[4,16,24,320]{3,2,1,0:T(8,128)} %fusion.113, f32[4,16,24,320]{3,2,1,0:T(8,128)} %fusion.116, f32[4,16,24,320]{3,2,1,0:T(8,128)} %fusion.162, f32[4,16,24,320]{3,2,1,0:T(8,128)} %fusion.119, ...), kind=kOutput, calls=%fused_computation.31 | output fusion | flops 9830400 | bytes 23101488 | tf_op jit(solution)/shard_map/jit(cumsum)/reduce_window_sum | solution.py:170
  411.9 51.7 %all-reduce.9.cloned.1.call-done = f32[3,3,320,320]{2,1,0,3:T(4,128)} async-done(((f32[3,3,320,320]{2,1,0,3:T(4,128)}), f32[3,3,320,320]{2,1,0,3:T(4,128)}) %all-reduce.9.cloned.1.call-update) | async-done | bytes 3686416
  465.7 33.7 %all-gather.6.cloned.1.call-done = f32[8,16,24,320]{3,2,1,0:T(8,128)} async-done(((f32[1,16,24,320]{3,2,1,0:T(8,128)}), f32[8,16,24,320]{3,2,1,0:T(8,128)}) %all-gather.6.cloned.1.call-update) | async-done | bytes 3932176 | tf_op jit(solution)/shard_map/all_gather | solution.py:18
  499.4 8.7 %while.43 = (s32[]{:T(128)}, f32[16,24,320]{2,1,0:T(8,128)S(1)}, s32[]{:T(128)}, f32[8,16,24,320]{3,2,1,0:T(8,128)}, s32[]{:T(128)}, /*index=5*/s32[]{:T(128)}) while((s32[]{:T(128)}, f32[16,24,320]{2,1,0:T(8,128)S(1)}, s32[]{:T(128)}, f32[8,16,24,320]{3,2,1,0:T(8,128)}, s32[]{:T(128)}, /*index=5*/s32[]{:T(128)}) %tuple.109), condition=%wide.region_19.20_spmd.clone, body=%wide.region_18.19_spmd.clone.sunk | while | flops 368644 | bytes 1474653 | solution.py:28
  508.1 3.4 add_add_fusion
  511.4 77.7 %all-reduce.7.cloned.1.call-done = f32[3,3,320,40]{2,1,0,3:T(4,128)} async-done(((f32[3,3,320,40]{2,1,0,3:T(4,128)}), f32[3,3,320,40]{2,1,0,3:T(4,128)}) %all-reduce.7.cloned.1.call-update) | async-done | bytes 460816 | tf_op jit(solution)/shard_map/psum | solution.py:190
  (257 shorter events, 173.8 us)
Async XLA Ops:
  7.2 61.3 %copy-start = (f32[1000,320]{0,1:T(8,128)S(1)}, f32[1000,320]{0,1:T(8,128)}, u32[]{:S(2)}) copy-start(f32[1000,320]{0,1:T(8,128)} %param.22) | copy-start | bytes 3840004
  7.2 62.9 %copy-start.2 = (f32[16,24,320]{2,1,0:T(8,128)S(1)}, f32[16,24,320]{2,1,0:T(8,128)}, u32[]{:S(2)}) copy-start(f32[16,24,320]{2,1,0:T(8,128)} %param.16) | copy-start | bytes 1474564
  7.2 142.0 %all-gather.4.cloned.1.call-start = ((), (), s32[]{:S(2)}) async-start(), calls=%async_computation | async-start | bytes 5308416 | tf_op jit(solution)/shard_map/all_gather | solution.py:18
  51.0 27.4 %copy-start.39 = (f32[4,320]{1,0:T(4,128)}, f32[4,320]{1,0:T(4,128)S(1)}, u32[]{:S(2)}) copy-start(f32[4,320]{1,0:T(4,128)S(1)} %sub.62) | copy-start | bytes 15364
  68.5 9.9 %copy-start.41 = (f32[4,320]{1,0:T(4,128)}, f32[4,320]{1,0:T(4,128)S(1)}, u32[]{:S(2)}) copy-start(f32[4,320]{1,0:T(4,128)S(1)} %mul.187) | copy-start | bytes 15364
  70.8 20.7 %copy-start.5 = (bf16[4,16,24,320]{3,2,1,0:T(8,128)(2,1)}, bf16[4,16,24,320]{3,2,1,0:T(8,128)(2,1)S(1)}, u32[]{:S(2)}) copy-start(bf16[4,16,24,320]{3,2,1,0:T(8,128)(2,1)S(1)} %fusion.17) | copy-start | bytes 2949124
  70.8 7.6 %collective-permute-start = (bf16[4,1,24,320]{3,2,1,0:T(8,128)(2,1)S(1)}, bf16[4,1,24,320]{3,2,1,0:T(8,128)(2,1)S(1)}, u32[]{:S(2)}, u32[]{:S(2)}) collective-permute-start(bf16[4,1,24,320]{3,2,1,0:T(8,128)(2,1)S(1)} %get-tuple-element.339), channel_id=1, source_target_pairs={{0,4},{4,8},{8,12},{1,5},{5,9},{9,13},{2,6},{6,10},{10,14},{3,7},{... | collective-permute-start | bytes 184328 | tf_op jit(solution)/shard_map/ppermute | solution.py:36
  74.5 6.2 %collective-permute-start.1 = (bf16[4,1,24,320]{3,2,1,0:T(8,128)(2,1)S(1)}, bf16[4,1,24,320]{3,2,1,0:T(8,128)(2,1)S(1)}, u32[]{:S(2)}, u32[]{:S(2)}) collective-permute-start(bf16[4,1,24,320]{3,2,1,0:T(8,128)(2,1)S(1)} %get-tuple-element.340), channel_id=1, source_target_pairs={{4,0},{8,4},{12,8},{5,1},{9,5},{13,9},{6,2},{10,6},{14,10},{7,3},{... | collective-permute-start | bytes 184328 | tf_op jit(solution)/shard_map/ppermute | solution.py:39
  78.4 13.1 %copy-start.32 = (bf16[4,1,24,320]{3,2,1,0:T(8,128)(2,1)}, bf16[4,1,24,320]{3,2,1,0:T(8,128)(2,1)S(1)}, u32[]{:S(2)}) copy-start(bf16[4,1,24,320]{3,2,1,0:T(8,128)(2,1)S(1)} %collective-permute-done) | copy-start | bytes 184324
  80.7 10.8 %copy-start.30 = (bf16[4,1,24,320]{3,2,1,0:T(8,128)(2,1)}, bf16[4,1,24,320]{3,2,1,0:T(8,128)(2,1)S(1)}, u32[]{:S(2)}) copy-start(bf16[4,1,24,320]{3,2,1,0:T(8,128)(2,1)S(1)} %collective-permute-done.1) | copy-start | bytes 184324
  80.9 7.7 %collective-permute-start.2 = (bf16[4,18,1,320]{3,2,1,0:T(2,128)(2,1)S(1)}, bf16[4,18,1,320]{3,2,1,0:T(2,128)(2,1)S(1)}, u32[]{:S(2)}, u32[]{:S(2)}) collective-permute-start(bf16[4,18,1,320]{3,2,1,0:T(2,128)(2,1)S(1)} %get-tuple-element.333), channel_id=1, source_target_pairs={{0,1},{1,2},{2,3},{4,5},{5,6},{6,7},{8,9},{9,10},{10,11},{12,13},{... | collective-permute-start | bytes 138248 | tf_op jit(solution)/shard_map/ppermute | solution.py:36
  84.8 6.6 %collective-permute-start.3 = (bf16[4,18,1,320]{3,2,1,0:T(2,128)(2,1)S(1)}, bf16[4,18,1,320]{3,2,1,0:T(2,128)(2,1)S(1)}, u32[]{:S(2)}, u32[]{:S(2)}) collective-permute-start(bf16[4,18,1,320]{3,2,1,0:T(2,128)(2,1)S(1)} %get-tuple-element.334), channel_id=1, source_target_pairs={{1,0},{2,1},{3,2},{5,4},{6,5},{7,6},{9,8},{10,9},{11,10},{13,12},{... | collective-permute-start | bytes 138248 | tf_op jit(solution)/shard_map/ppermute | solution.py:39
  92.6 10.8 %copy-start.13 = (bf16[4,18,25,320]{3,2,1,0:T(8,128)(2,1)}, bf16[4,18,25,320]{3,2,1,0:T(8,128)(2,1)S(1)}, u32[]{:S(2)}) copy-start(bf16[4,18,25,320]{3,2,1,0:T(8,128)(2,1)S(1)} %get-tuple-element.331) | copy-start | bytes 3456004
  114.5 230.3 %all-gather.8.cloned.1.call-start = ((), (), s32[]{:S(2)}) async-start(), calls=%async_computation.2 | async-start | bytes 5308416 | tf_op jit(solution)/shard_map/all_gather | solution.py:18
  114.9 18.0 %copy-start.7 = (bf16[4,16,24,320]{3,2,1,0:T(8,128)(2,1)}, bf16[4,16,24,320]{3,2,1,0:T(8,128)(2,1)S(1)}, u32[]{:S(2)}) copy-start(bf16[4,16,24,320]{3,2,1,0:T(8,128)(2,1)S(1)} %multiply_convert_fusion) | copy-start | bytes 2949124
  114.9 6.9 %collective-permute-start.8 = (bf16[4,1,24,320]{3,2,1,0:T(8,128)(2,1)S(1)}, bf16[4,1,24,320]{3,2,1,0:T(8,128)(2,1)S(1)}, u32[]{:S(2)}, u32[]{:S(2)}) collective-permute-start(bf16[4,1,24,320]{3,2,1,0:T(8,128)(2,1)S(1)} %get-tuple-element.336), channel_id=1, source_target_pairs={{0,4},{4,8},{8,12},{1,5},{5,9},{9,13},{2,6},{6,10},{10,14},{3,7},{... | collective-permute-start | bytes 184328 | tf_op jit(solution)/shard_map/ppermute | solution.py:36
  117.2 6.2 %collective-permute-start.9 = (bf16[4,1,24,320]{3,2,1,0:T(8,128)(2,1)S(1)}, bf16[4,1,24,320]{3,2,1,0:T(8,128)(2,1)S(1)}, u32[]{:S(2)}, u32[]{:S(2)}) collective-permute-start(bf16[4,1,24,320]{3,2,1,0:T(8,128)(2,1)S(1)} %get-tuple-element.335), channel_id=1, source_target_pairs={{4,0},{8,4},{12,8},{5,1},{9,5},{13,9},{6,2},{10,6},{14,10},{7,3},{... | collective-permute-start | bytes 184328 | tf_op jit(solution)/shard_map/ppermute | solution.py:39
  121.8 11.1 %copy-start.10 = (bf16[3,3,320,320]{3,2,1,0:T(8,128)(2,1)S(1)}, bf16[3,3,320,320]{3,2,1,0:T(8,128)(2,1)}, u32[]{:S(2)}) copy-start(bf16[3,3,320,320]{3,2,1,0:T(8,128)(2,1)} %param.24) | copy-start | bytes 5529604
  121.9 11.0 %copy-start.34 = (bf16[4,1,24,320]{3,2,1,0:T(8,128)(2,1)}, bf16[4,1,24,320]{3,2,1,0:T(8,128)(2,1)S(1)}, u32[]{:S(2)}) copy-start(bf16[4,1,24,320]{3,2,1,0:T(8,128)(2,1)S(1)} %collective-permute-done.8) | copy-start | bytes 184324
  123.5 9.4 %copy-start.36 = (bf16[4,1,24,320]{3,2,1,0:T(8,128)(2,1)}, bf16[4,1,24,320]{3,2,1,0:T(8,128)(2,1)S(1)}, u32[]{:S(2)}) copy-start(bf16[4,1,24,320]{3,2,1,0:T(8,128)(2,1)S(1)} %collective-permute-done.9) | copy-start | bytes 184324
  123.7 11.8 %collective-permute-start.10 = (bf16[4,18,1,320]{3,2,1,0:T(2,128)(2,1)S(1)}, bf16[4,18,1,320]{3,2,1,0:T(2,128)(2,1)S(1)}, u32[]{:S(2)}, u32[]{:S(2)}) collective-permute-start(bf16[4,18,1,320]{3,2,1,0:T(2,128)(2,1)S(1)} %get-tuple-element.326), channel_id=1, source_target_pairs={{1,0},{2,1},{3,2},{5,4},{6,5},{7,6},{9,8},{10,9},{11,10},{13,12},{... | collective-permute-start | bytes 138248 | tf_op jit(solution)/shard_map/ppermute | solution.py:39
  125.0 10.5 %collective-permute-start.11 = (bf16[4,18,1,320]{3,2,1,0:T(2,128)(2,1)S(1)}, bf16[4,18,1,320]{3,2,1,0:T(2,128)(2,1)S(1)}, u32[]{:S(2)}, u32[]{:S(2)}) collective-permute-start(bf16[4,18,1,320]{3,2,1,0:T(2,128)(2,1)S(1)} %get-tuple-element.325), channel_id=1, source_target_pairs={{0,1},{1,2},{2,3},{4,5},{5,6},{6,7},{8,9},{9,10},{10,11},{12,13},{... | collective-permute-start | bytes 138248 | tf_op jit(solution)/shard_map/ppermute | solution.py:36
  295.8 9.1 %copy-start.44 = (f32[4]{0:T(128)S(1)}, f32[4]{0:T(128)}, u32[]{:S(2)}) copy-start(f32[4]{0:T(128)} %param.19) | copy-start | bytes 52
  299.9 163.7 %all-reduce.9.cloned.1.call-start = ((), (), s32[]{:S(2)}) async-start(), calls=%async_computation.4 | async-start | bytes 11796480
  301.5 14.3 %collective-permute-start.4 = (bf16[4,1,24,320]{3,2,1,0:T(8,128)(2,1)}, bf16[4,1,24,320]{3,2,1,0:T(8,128)(2,1)}, u32[]{:S(2)}, u32[]{:S(2)}) collective-permute-start(bf16[4,1,24,320]{3,2,1,0:T(8,128)(2,1)} %get-tuple-element.337), channel_id=1, source_target_pairs={{0,4},{4,8},{8,12},{1,5},{5,9},{9,13},{2,6},{6,10},{10,14},{3,7},{... | collective-permute-start | bytes 184328 | tf_op jit(solution)/shard_map/ppermute | solution.py:36
  303.5 12.4 %collective-permute-start.5 = (bf16[4,1,24,320]{3,2,1,0:T(8,128)(2,1)}, bf16[4,1,24,320]{3,2,1,0:T(8,128)(2,1)}, u32[]{:S(2)}, u32[]{:S(2)}) collective-permute-start(bf16[4,1,24,320]{3,2,1,0:T(8,128)(2,1)} %get-tuple-element.338), channel_id=1, source_target_pairs={{4,0},{8,4},{12,8},{5,1},{9,5},{13,9},{6,2},{10,6},{14,10},{7,3},{... | collective-permute-start | bytes 184328 | tf_op jit(solution)/shard_map/ppermute | solution.py:39
  317.3 13.1 %collective-permute-start.6 = (bf16[4,18,1,320]{3,2,1,0:T(2,128)(2,1)S(1)}, bf16[4,18,1,320]{3,2,1,0:T(2,128)(2,1)S(1)}, u32[]{:S(2)}, u32[]{:S(2)}) collective-permute-start(bf16[4,18,1,320]{3,2,1,0:T(2,128)(2,1)S(1)} %get-tuple-element.329), channel_id=1, source_target_pairs={{0,1},{1,2},{2,3},{4,5},{5,6},{6,7},{8,9},{9,10},{10,11},{12,13},{... | collective-permute-start | bytes 138248 | tf_op jit(solution)/shard_map/ppermute | solution.py:36
  318.6 11.8 %collective-permute-start.7 = (bf16[4,18,1,320]{3,2,1,0:T(2,128)(2,1)S(1)}, bf16[4,18,1,320]{3,2,1,0:T(2,128)(2,1)S(1)}, u32[]{:S(2)}, u32[]{:S(2)}) collective-permute-start(bf16[4,18,1,320]{3,2,1,0:T(2,128)(2,1)S(1)} %get-tuple-element.330), channel_id=1, source_target_pairs={{1,0},{2,1},{3,2},{5,4},{6,5},{7,6},{9,8},{10,9},{11,10},{13,12},{... | collective-permute-start | bytes 138248 | tf_op jit(solution)/shard_map/ppermute | solution.py:39
  381.7 117.7 %all-gather.6.cloned.1.call-start = ((), (), s32[]{:S(2)}) async-start(), calls=%async_computation.1 | async-start | bytes 5308416 | tf_op jit(solution)/shard_map/all_gather | solution.py:18
  399.7 11.0 %copy-start.49 = (u32[128]{0:T(128)S(1)}, u32[128]{0:T(128)}, u32[]{:S(2)}) copy-start(u32[128]{0:T(128)} %constant.115) | copy-start | bytes 1540
  410.6 178.6 %all-reduce.7.cloned.1.call-start = ((), (), s32[]{:S(2)}) async-start(), calls=%async_computation.3 | async-start | bytes 1474560 | tf_op jit(solution)/shard_map/psum | solution.py:190
  508.1 83.0 %copy-start.1 = (f32[1000,320]{0,1:T(8,128)S(1)}, f32[1000,320]{0,1:T(8,128)}, u32[]{:S(2)}) copy-start(f32[1000,320]{0,1:T(8,128)} %param.22) | copy-start | bytes 3840004
  (35 other events, 116.5 us)
Sparse Core Ops, SparseCore 0:
  114.6 32.3 all-gather.3
  300.0 29.2 all-gather.7
  381.8 81.6 all-reduce.8
  465.2 34.1 all-gather.5
  502.9 86.2 all-reduce.6
